TPU v7x, 256 devices: a whole 4x4x8 slice. The times are simulated.
256 devices in a mesh: tm: 8 (over x, core), tile: 32 (over y, z).
Axes of the slice: x: 4, y: 4, z: 8, core: 2. Of those that a mesh axis runs over, the one named last changes fastest.
Arguments:
- recording: bfloat16 [262144, 1024], P('tile', 'tm'), may hold values from -300 to 300
- footprints: bfloat16 [262144, 256], P('tile'), may hold values from -0.375 to 0.375
- pattern: int32 [1024, 4], P('tile'), may hold values from 0 to 35, as said below
- decay: float32 [65536], P('tile'), may hold values from 0.96 to 1
- frame_gain: float32 [1024], P('tm'), may hold values from 0.6 to 1
- spikes: float32 [65536, 1024], P('tile', 'tm'), may hold values from 0 to 0.15
Outputs:
- spikes_out: float32 [65536, 1024], P('tile', 'tm')
- traces_last: float32 [65536, 1024], P('tile', 'tm')
Inputs may be any that keep to these rules, and one draw needn't show every extreme that they name: `pattern`: with p = q % 32, row q holds 4 different values between p and p + 4, always including p, p + 2 and p + 4, in some order; value v names the stripe's own neuron block v - 2, so values under 2 or over 2048 // 64 + 1 name edge blocks of the adjacent stripes.
All inputs are finite; a program needn't handle non-finite values.
Results may differ from a plain program's by a relative error of at most 0.00073.
Values may be sent and summed in bfloat16 or wider, within the bound.
A program may use at most 128 MiB of HBM per device.

v0:
```python
import jax
import jax.numpy as jnp
from jax import lax
from jax.sharding import PartitionSpec as P

NEU_BLOCK = 64
PIX_BLOCK = 256
K = 4
HB = 2
ITERS = 2


def entering(array, axis, combine, identity, reverse):
    length, place = (lax.axis_size(axis), lax.axis_index(axis))
    everything = jax.tree.map(lambda part: lax.all_gather(part, axis), array)
    start = jax.tree.map(
        lambda part, zero: jnp.broadcast_to(jnp.asarray(zero, part.dtype), part.shape),
        array,
        identity,
    )

    def turn(k, before):
        at = length - 1 - k if reverse else k
        reached = at > place if reverse else at < place
        new = combine(before, jax.tree.map(lambda part: part[at], everything))
        return jax.tree.map(lambda a, b: jnp.where(reached, a, b), new, before)

    return lax.fori_loop(0, length, turn, start)


def padded(array, sides, width):
    for axis, dim in sides:
        size, length = (lax.axis_size(axis), array.shape[dim])
        up = [(i, (i + 1) % size) for i in range(size - 1)]
        down = [(j, i) for i, j in up]
        last = lax.slice_in_dim(array, length - width, length, axis=dim)
        initial = lax.slice_in_dim(array, 0, width, axis=dim)
        before = lax.ppermute(last, axis, up)
        after = lax.ppermute(initial, axis, down)
        array = jnp.concatenate([before, array, after], axis=dim)
    return array


def shifted(array, axis, by):
    length = lax.axis_size(axis)
    pairs = [(i, i + by) for i in range(length) if 0 <= i + by < length]
    return lax.ppermute(array, axis, pairs)


def chain_affine(earlier, latter):
    return (earlier[0] * latter[0], latter[0] * earlier[1] + latter[1])


def tri_matmul(values, table):
    return jnp.dot(
        values, table, precision=lax.Precision.HIGHEST, preferred_element_type=jnp.float32
    )


def incoming_forward(summary):
    result = entering(
        summary, "tm", chain_affine, (jnp.ones_like(summary[0]), jnp.zeros_like(summary[1])), False
    )
    return result[1]


def incoming_backward(summary):
    result = entering(
        summary, "tm", chain_affine, (jnp.ones_like(summary[0]), jnp.zeros_like(summary[1])), True
    )
    return result[1]


def per_device(recording, footprints, pattern, decay, frame_gain, spikes):
    neurons, frames = spikes.shape
    blocks = neurons // NEU_BLOCK
    rim_rows = HB * NEU_BLOCK
    drive_gain = jnp.sqrt(1.0 - decay * decay)[:, None]
    decay_rate = decay[:, None] * frame_gain[None, :]
    back_rate = jnp.concatenate(
        [decay[:, None] * frame_gain[None, 1:], jnp.ones((neurons, 1), jnp.float32)], axis=1
    )
    foot_blocks = footprints.reshape(blocks, PIX_BLOCK, K * NEU_BLOCK)
    record = recording.astype(jnp.float32)
    row_pos = lax.broadcasted_iota(jnp.int32, (frames, frames), 0)
    col_pos = lax.broadcasted_iota(jnp.int32, (frames, frames), 1)
    upper_incl = (row_pos <= col_pos).astype(jnp.float32)
    upper_strict = (row_pos < col_pos).astype(jnp.float32)
    lower_incl = (row_pos >= col_pos).astype(jnp.float32)
    fwd_total = jnp.exp(tri_matmul(jnp.log(decay_rate), upper_incl))
    back_log = tri_matmul(jnp.log(back_rate), upper_strict)
    back_prefix = jnp.exp(back_log)
    back_total = jnp.exp(back_log[:, -1:] - back_log)
    wide_onehot = (
        pattern.reshape(1, -1) == jnp.arange(blocks + 2 * HB, dtype=jnp.int32)[:, None]
    ).astype(jnp.float32)

    def forward_pass(drive):
        local_part = fwd_total * tri_matmul(drive / fwd_total, upper_incl)
        carry_in = incoming_forward((fwd_total[:, -1], local_part[:, -1]))
        return local_part + fwd_total * carry_in[:, None]

    def footprint_apply(values):
        extended = padded(values, (("tile", 0),), rim_rows)
        picked = extended.reshape(blocks + 2 * HB, NEU_BLOCK, frames)[pattern]
        picked = picked.reshape(blocks, K * NEU_BLOCK, frames)
        fitted = jnp.einsum("paj,pjf->paf", foot_blocks, picked, preferred_element_type=jnp.float32)
        return fitted.reshape(blocks * PIX_BLOCK, frames)

    current = spikes
    traces = spikes
    for iteration in range(ITERS):
        traces = forward_pass(drive_gain * current)
        fitted = footprint_apply(traces.astype(jnp.bfloat16))
        residual = (fitted - record).astype(jnp.bfloat16)
        contrib = jnp.einsum(
            "paj,paf->pjf",
            foot_blocks,
            residual.reshape(blocks, PIX_BLOCK, frames),
            preferred_element_type=jnp.float32,
        )
        contrib = contrib.reshape(blocks * K, NEU_BLOCK * frames)
        summed = jnp.dot(
            wide_onehot,
            contrib,
            precision=lax.Precision.HIGHEST,
            preferred_element_type=jnp.float32,
        )
        summed = summed.reshape(neurons + 2 * rim_rows, frames)
        from_above = shifted(summed[:rim_rows], "tile", -1)
        from_below = shifted(summed[rim_rows + neurons :], "tile", 1)
        own_sums = summed[rim_rows : rim_rows + neurons]
        own_sums = own_sums.at[:rim_rows].add(from_below)
        backward_local_part = (
            tri_matmul(own_sums.at[neurons - rim_rows :].add(from_above) * back_prefix, lower_incl)
            / back_prefix
        )
        head = decay_rate[:, 0]
        backward_carry_in = incoming_backward(
            (head * back_total[:, 0], head * backward_local_part[:, 0])
        )
        gradient = drive_gain * (backward_local_part + back_total * backward_carry_in[:, None])
        direction = forward_pass(drive_gain * gradient).astype(jnp.bfloat16)
        projected = footprint_apply(direction)
        grad_sq, image_sq = lax.psum(
            (jnp.sum(gradient * gradient), jnp.sum(projected * projected)), ("tm", "tile")
        )
        step_size = grad_sq / (image_sq + 1e-06)
        current = jnp.maximum(current - step_size * gradient, 0.0)
    return (current, traces)


def solution(mesh):
    return jax.shard_map(
        per_device,
        mesh=mesh,
        in_specs=(
            P("tile", "tm"),
            P("tile", None),
            P("tile", None),
            P("tile"),
            P("tm"),
            P("tile", "tm"),
        ),
        out_specs=(P("tile", "tm"), P("tile", "tm")),
        check_vma=False,
    )
```

profile of v0, /device:TPU:1, one launch (start us, length us, event | category | flops | bytes accessed | tf_op | source)
XLA Modules:
  0.0 472.5 jit_solution(6232184334555677830)
XLA Ops:
  6.4 15.9 %all-gather.1 = f32[16384,1]{0,1:T(1,128)S(1)} all-gather(f32[2048,1]{0,1:T(1,128)S(1)} %slice.222), channel_id=3, replica_groups=mesh['tm'=8,'tile'=32] {'tm'}, dimensions={0}, use_global_device_ids=true | all-gather | bytes 73728 | tf_op jit(solution)/shard_map/all_gather | solution.py:15
  23.6 12.8 %all-gather = f32[16384,1]{0,1:T(1,128)S(1)} all-gather(f32[2048,1]{0,1:T(1,128)S(1)} %slice.221), channel_id=2, replica_groups=mesh['tm'=8,'tile'=32] {'tm'}, dimensions={0}, use_global_device_ids=true | all-gather | bytes 73728 | tf_op jit(solution)/shard_map/all_gather | solution.py:15
  39.1 2.2 collective-permute-start
  46.5 2.2 gather_fusion
  48.6 6.3 %convolution_bitcast_fusion.3 = f32[32,256,128]{1,2,0:T(8,128)} fusion(bf16[32,256,128]{2,1,0:T(8,128)(2,1)} %bitcast.92, bf16[32,256,256]{2,1,0:T(8,128)(2,1)} %bitcast.82), kind=kOutput, calls=%fused_computation.38 | convolution fusion | flops 536870912 | bytes 10485760 | tf_op jit(solution)/shard_map/paj,pjf->paf/dot_general | solution.py:107
  54.9 5.6 %copy.21 = f32[32,256,128]{2,1,0:T(8,128)} copy(f32[32,256,128]{1,2,0:T(8,128)} %convolution_bitcast_fusion.3) | data formatting | bytes 8388608 | tf_op jit(solution)/shard_map/paj,pjf->paf/dot_general | solution.py:107
  60.5 3.4 fusion
  64.6 2.9 convolution_bitcast_fusion.2
  67.4 5.6 %copy.23 = f32[32,256,128]{2,1,0:T(8,128)} copy(f32[32,256,128]{1,2,0:T(8,128)} %convolution_bitcast_fusion.2) | data formatting | bytes 8388608 | tf_op jit(solution)/shard_map/paj,paf->pjf/dot_general | solution.py:116
  73.0 5.0 %reshape.231 = f32[128,8192]{1,0:T(8,128)} reshape(f32[32,256,128]{2,1,0:T(8,128)} %copy.23) | data formatting | bytes 8388608 | tf_op jit(solution)/shard_map/reshape | solution.py:122
  78.0 3.8 fusion.25
  84.2 4.3 collective-permute-start.2
  88.5 1.8 broadcast_multiply_fusion.1
  97.3 2.8 collective-permute-done.3
  101.6 2.2 convolution_divide_fusion.1
  104.7 15.1 %all-gather.3 = f32[16384,1]{0,1:T(1,128)S(1)} all-gather(f32[2048,1]{0,1:T(1,128)S(1)} %get-tuple-element.896), channel_id=5, replica_groups=mesh['tm'=8,'tile'=32] {'tm'}, dimensions={0}, use_global_device_ids=true | all-gather | bytes 73728 | tf_op jit(solution)/shard_map/all_gather | solution.py:15
  120.6 12.8 %all-gather.2 = f32[16384,1]{0,1:T(1,128)S(1)} all-gather(f32[2048,1]{0,1:T(1,128)S(1)} %get-tuple-element.897), channel_id=4, replica_groups=mesh['tm'=8,'tile'=32] {'tm'}, dimensions={0}, use_global_device_ids=true | all-gather | bytes 73728 | tf_op jit(solution)/shard_map/all_gather | solution.py:15
  138.6 12.7 %all-gather.4 = f32[16384,1]{0,1:T(1,128)S(1)} all-gather(f32[2048,1]{0,1:T(1,128)S(1)} %slice.234), channel_id=6, replica_groups=mesh['tm'=8,'tile'=32] {'tm'}, dimensions={0}, use_global_device_ids=true | all-gather | bytes 73728 | tf_op jit(solution)/shard_map/all_gather | solution.py:15
  154.0 4.8 %collective-permute-start.4 = (bf16[128,128]{0,1:T(8,128)(2,1)S(1)}, bf16[128,128]{0,1:T(8,128)(2,1)S(1)}, u32[]{:S(2)}, u32[]{:S(2)}) collective-permute-start(bf16[128,128]{0,1:T(8,128)(2,1)S(1)} %get-tuple-element.902), channel_id=1, source_target_pairs={{0,1},{1,2},{2,3},{3,4},{4,5},{5,6},{6,7},{7,8},{8,9},{9,10},{10,1... | collective-permute-start | bytes 98312 | tf_op jit(solution)/shard_map/ppermute | solution.py:38
  160.2 3.6 collective-permute-done.5
  164.2 2.2 gather_fusion.1
  166.3 5.0 %multiply_reduce_fusion.1 = f32[]{:T(128)} fusion(bf16[32,256,128]{2,1,0:T(8,128)(2,1)} %bitcast.97, bf16[32,256,256]{2,1,0:T(8,128)(2,1)} %bitcast.83), kind=kOutput, calls=%fused_computation.27 | convolution fusion | flops 538968064 | bytes 6291460 | tf_op jit(solution)/shard_map/paj,pjf->paf/dot_general | solution.py:107
  171.3 78.7 %all-reduce.2 = (f32[]{:T(128)}, f32[]{:T(128)}) all-reduce(f32[]{:T(128)} %get-tuple-element.876, f32[]{:T(128)} %multiply_reduce_fusion.1), channel_id=1, replica_groups=mesh['tm'=8,'tile'=32] {'tm','tile'}, use_global_device_ids=true, to_apply=%region_5.6 | all-reduce | flops 2 | bytes 16 | tf_op jit(solution)/shard_map/psum | solution.py:145
  251.3 2.1 convolution_multiply_fusion.1
  254.5 13.2 %all-gather.5 = f32[16384,1]{0,1:T(1,128)S(1)} all-gather(f32[2048,1]{0,1:T(1,128)S(1)} %slice.237), channel_id=7, replica_groups=mesh['tm'=8,'tile'=32] {'tm'}, dimensions={0}, use_global_device_ids=true | all-gather | bytes 73728 | tf_op jit(solution)/shard_map/all_gather | solution.py:15
  269.0 2.4 fusion.30
  271.4 2.1 collective-permute-start.6
  275.0 3.1 collective-permute-done.7
  278.5 2.2 gather_fusion.2
  280.7 6.3 %convolution_bitcast_fusion.1 = f32[32,256,128]{1,2,0:T(8,128)} fusion(bf16[32,256,128]{2,1,0:T(8,128)(2,1)} %bitcast.93, bf16[32,256,256]{2,1,0:T(8,128)(2,1)} %bitcast.84), kind=kOutput, calls=%fused_computation.36 | convolution fusion | flops 536870912 | bytes 10485760 | tf_op jit(solution)/shard_map/paj,pjf->paf/dot_general | solution.py:107
  287.0 5.6 %copy.33 = f32[32,256,128]{2,1,0:T(8,128)} copy(f32[32,256,128]{1,2,0:T(8,128)} %convolution_bitcast_fusion.1) | data formatting | bytes 8388608 | tf_op jit(solution)/shard_map/paj,pjf->paf/dot_general | solution.py:107
  292.6 3.4 fusion.1
  296.6 2.9 convolution_bitcast_fusion
  299.5 5.6 %copy.35 = f32[32,256,128]{2,1,0:T(8,128)} copy(f32[32,256,128]{1,2,0:T(8,128)} %convolution_bitcast_fusion) | data formatting | bytes 8388608 | tf_op jit(solution)/shard_map/paj,paf->pjf/dot_general | solution.py:116
  305.1 5.0 %reshape.239 = f32[128,8192]{1,0:T(8,128)} reshape(f32[32,256,128]{2,1,0:T(8,128)} %copy.35) | data formatting | bytes 8388608 | tf_op jit(solution)/shard_map/reshape | solution.py:122
  310.1 3.8 fusion.24
  317.7 2.6 collective-permute-start.8
  327.3 2.2 collective-permute-done.9
  331.0 2.2 convolution_divide_fusion
  335.0 15.6 %all-gather.6 = f32[16384,1]{0,1:T(1,128)S(1)} all-gather(f32[2048,1]{0,1:T(1,128)S(1)} %slice_multiply_fusion), channel_id=8, replica_groups=mesh['tm'=8,'tile'=32] {'tm'}, dimensions={0}, use_global_device_ids=true | all-gather | bytes 73728 | tf_op jit(solution)/shard_map/all_gather | solution.py:15
  352.0 2.1 multiply_reduce_fusion.2
  356.0 12.9 %all-gather.7 = f32[16384,1]{0,1:T(1,128)S(1)} all-gather(f32[2048,1]{0,1:T(1,128)S(1)} %slice.246), channel_id=9, replica_groups=mesh['tm'=8,'tile'=32] {'tm'}, dimensions={0}, use_global_device_ids=true | all-gather | bytes 73728 | tf_op jit(solution)/shard_map/all_gather | solution.py:15
  372.4 4.0 collective-permute-start.10
  379.3 2.1 collective-permute-done.11
  381.7 2.2 gather_fusion.3
  383.9 5.1 %multiply_reduce_fusion = f32[]{:T(128)} fusion(bf16[32,256,128]{2,1,0:T(8,128)(2,1)} %bitcast.96, bf16[32,256,256]{2,1,0:T(8,128)(2,1)} %bitcast.85), kind=kOutput, calls=%fused_computation.26 | convolution fusion | flops 538968064 | bytes 6291460 | tf_op jit(solution)/shard_map/paj,pjf->paf/dot_general | solution.py:107
  389.0 78.4 %all-reduce.1 = (f32[]{:T(128)}, f32[]{:T(128)}) all-reduce(f32[]{:T(128)} %get-tuple-element.872, f32[]{:T(128)} %multiply_reduce_fusion), channel_id=1, replica_groups=mesh['tm'=8,'tile'=32] {'tm','tile'}, use_global_device_ids=true, to_apply=%region_15.16 | all-reduce | flops 2 | bytes 16 | tf_op jit(solution)/shard_map/psum | solution.py:145
  470.0 2.5 copy.42
  (264 shorter events, 68.6 us)
Async XLA Ops:
  1.3 4.0 copy-start.25
  4.5 19.1 %copy-start.2 = (f32[2048,128]{0,1:T(8,128)}, f32[2048,128]{0,1:T(8,128)S(1)}, u32[]{:S(2)}) copy-start(f32[2048,128]{0,1:T(8,128)S(1)} %copy.30) | copy-start | bytes 3145732
  5.4 1.0 copy-start.12
  6.4 36.2 %copy-start.29 = (f32[128]{0:T(128)S(1)}, f32[128]{0:T(128)}, u32[]{:S(2)}) copy-start(f32[128]{0:T(128)} %param.30) | copy-start | bytes 1540
  6.4 36.3 %copy-start.28 = (s32[32,4]{0,1:T(4,128)S(1)}, s32[32,4]{0,1:T(4,128)}, u32[]{:S(2)}) copy-start(s32[32,4]{0,1:T(4,128)} %param.28) | copy-start | bytes 1540
  6.4 36.5 %copy-start.21 = (f32[2048]{0:T(1024)S(1)}, f32[2048]{0:T(1024)}, u32[]{:S(2)}) copy-start(f32[2048]{0:T(1024)} %param.29) | copy-start | bytes 24580
  39.1 6.3 %collective-permute-start = (bf16[128,128]{0,1:T(8,128)(2,1)S(1)}, bf16[128,128]{0,1:T(8,128)(2,1)S(1)}, u32[]{:S(2)}, u32[]{:S(2)}) collective-permute-start(bf16[128,128]{0,1:T(8,128)(2,1)S(1)} %get-tuple-element.904), channel_id=1, source_target_pairs={{0,1},{1,2},{2,3},{3,4},{4,5},{5,6},{6,7},{7,8},{8,9},{9,10},{10,1... | collective-permute-start | bytes 98312 | tf_op jit(solution)/shard_map/ppermute | solution.py:38
  41.2 4.8 %collective-permute-start.1 = (bf16[128,128]{0,1:T(8,128)(2,1)S(1)}, bf16[128,128]{0,1:T(8,128)(2,1)S(1)}, u32[]{:S(2)}, u32[]{:S(2)}) collective-permute-start(bf16[128,128]{0,1:T(8,128)(2,1)S(1)} %get-tuple-element.905), channel_id=1, source_target_pairs={{1,0},{2,1},{3,2},{4,3},{5,4},{6,5},{7,6},{8,7},{9,8},{10,9},{11,1... | collective-permute-start | bytes 98312 | tf_op jit(solution)/shard_map/ppermute | solution.py:39
  44.0 2.4 copy-start.22
  60.5 4.0 copy-start
  84.2 7.1 %copy-start.20 = (f32[2,8192]{1,0:T(2,128)S(1)}, f32[2,8192]{1,0:T(2,128)}, u32[]{:S(2)}) copy-start(f32[2,8192]{1,0:T(2,128)} %get-tuple-element.895) | copy-start | bytes 196612
  84.2 11.7 %collective-permute-start.2 = (f32[128,128]{0,1:T(8,128)}, f32[128,128]{0,1:T(8,128)}, u32[]{:S(2)}, u32[]{:S(2)}) collective-permute-start(f32[128,128]{0,1:T(8,128)} %copy.24), channel_id=1, source_target_pairs={{0,1},{1,2},{2,3},{3,4},{4,5},{5,6},{6,7},{7,8},{8,9},{9,10},{10,1... | collective-permute-start | bytes 196616 | tf_op jit(solution)/shard_map/ppermute | solution.py:47
  91.5 2.7 copy-start.17
  94.4 5.8 %collective-permute-start.3 = (f32[128,128]{0,1:T(8,128)S(1)}, f32[128,128]{0,1:T(8,128)S(1)}, u32[]{:S(2)}, u32[]{:S(2)}) collective-permute-start(f32[128,128]{0,1:T(8,128)S(1)} %copy.27), channel_id=1, source_target_pairs={{1,0},{2,1},{3,2},{4,3},{5,4},{6,5},{7,6},{8,7},{9,8},{10,9},{11,1... | collective-permute-start | bytes 196616 | tf_op jit(solution)/shard_map/ppermute | solution.py:47
  101.6 32.5 %copy-start.15 = (f32[2048]{0:T(1024)S(1)}, f32[2048]{0:T(1024)}, u32[]{:S(2)}) copy-start(f32[2048]{0:T(1024)} %custom-call.1) | copy-start | bytes 24580
  101.6 33.1 %copy-start.23 = (f32[2048,1]{0,1:T(1,128)S(1)}, f32[2048,1]{0,1:T(1,128)}, u32[]{:S(2)}) copy-start(f32[2048,1]{0,1:T(1,128)} %copy-done.22) | copy-start | bytes 24580
  101.6 33.1 %copy-start.26 = (f32[2048]{0:T(1024)S(1)}, f32[2048]{0:T(1024)}, u32[]{:S(2)}) copy-start(f32[2048]{0:T(1024)} %copy-done.25) | copy-start | bytes 24580
  135.7 1.0 copy-start.5
  137.6 1.0 copy-start.14
  154.0 6.2 %collective-permute-start.4 = (bf16[128,128]{0,1:T(8,128)(2,1)S(1)}, bf16[128,128]{0,1:T(8,128)(2,1)S(1)}, u32[]{:S(2)}, u32[]{:S(2)}) collective-permute-start(bf16[128,128]{0,1:T(8,128)(2,1)S(1)} %get-tuple-element.902), channel_id=1, source_target_pairs={{0,1},{1,2},{2,3},{3,4},{4,5},{5,6},{6,7},{7,8},{8,9},{9,10},{10,1... | collective-permute-start | bytes 98312 | tf_op jit(solution)/shard_map/ppermute | solution.py:38
  158.9 4.9 %collective-permute-start.5 = (bf16[128,128]{0,1:T(8,128)(2,1)S(1)}, bf16[128,128]{0,1:T(8,128)(2,1)S(1)}, u32[]{:S(2)}, u32[]{:S(2)}) collective-permute-start(bf16[128,128]{0,1:T(8,128)(2,1)S(1)} %get-tuple-element.903), channel_id=1, source_target_pairs={{1,0},{2,1},{3,2},{4,3},{5,4},{6,5},{7,6},{8,7},{9,8},{10,9},{11,1... | collective-permute-start | bytes 98312 | tf_op jit(solution)/shard_map/ppermute | solution.py:39
  166.3 85.0 %copy-start.3 = (f32[2048,128]{0,1:T(8,128)S(1)}, f32[2048,128]{0,1:T(8,128)}, u32[]{:S(2)}) copy-start(f32[2048,128]{0,1:T(8,128)} %copy-done.2) | copy-start | bytes 3145732
  253.5 1.0 copy-start.10
  271.4 3.6 collective-permute-start.6
  273.5 4.7 collective-permute-start.7
  292.6 4.0 copy-start.1
  317.7 8.1 %collective-permute-start.8 = (f32[128,128]{0,1:T(8,128)}, f32[128,128]{0,1:T(8,128)}, u32[]{:S(2)}, u32[]{:S(2)}) collective-permute-start(f32[128,128]{0,1:T(8,128)} %copy.36), channel_id=1, source_target_pairs={{0,1},{1,2},{2,3},{3,4},{4,5},{5,6},{6,7},{7,8},{8,9},{9,10},{10,1... | collective-permute-start | bytes 196616 | tf_op jit(solution)/shard_map/ppermute | solution.py:47
  321.4 2.8 copy-start.19
  321.4 2.9 copy-start.18
  324.5 5.0 %collective-permute-start.9 = (f32[128,128]{0,1:T(8,128)S(1)}, f32[128,128]{0,1:T(8,128)S(1)}, u32[]{:S(2)}, u32[]{:S(2)}) collective-permute-start(f32[128,128]{0,1:T(8,128)S(1)} %copy.39), channel_id=1, source_target_pairs={{1,0},{2,1},{3,2},{4,3},{5,4},{6,5},{7,6},{8,7},{9,8},{10,9},{11,1... | collective-permute-start | bytes 196616 | tf_op jit(solution)/shard_map/ppermute | solution.py:47
  331.0 20.4 %copy-start.16 = (f32[2048]{0:T(1024)S(1)}, f32[2048]{0:T(1024)}, u32[]{:S(2)}) copy-start(f32[2048]{0:T(1024)} %custom-call.4) | copy-start | bytes 24580
  331.0 21.0 %copy-start.24 = (f32[2048,1]{0,1:T(1,128)S(1)}, f32[2048,1]{0,1:T(1,128)}, u32[]{:S(2)}) copy-start(f32[2048,1]{0,1:T(1,128)} %copy-done.22) | copy-start | bytes 24580
  331.0 21.0 %copy-start.27 = (f32[2048]{0:T(1024)S(1)}, f32[2048]{0:T(1024)}, u32[]{:S(2)}) copy-start(f32[2048]{0:T(1024)} %copy-done.25) | copy-start | bytes 24580
  333.2 1.0 copy-start.11
  355.0 1.0 copy-start.13
  356.0 22.0 %copy-start.7 = (f32[2048,128]{0,1:T(8,128)S(1)}, f32[2048,128]{0,1:T(8,128)}, u32[]{:S(2)}) copy-start(f32[2048,128]{0,1:T(8,128)} %get-tuple-element.875) | copy-start | bytes 3145732
  371.6 0.8 copy-start.8
  372.4 9.0 %copy-start.9 = (bf16[2048,128]{0,1:T(8,128)(2,1)S(1)}, bf16[2048,128]{0,1:T(8,128)(2,1)}, u32[]{:S(2)}) copy-start(bf16[2048,128]{0,1:T(8,128)(2,1)} %copy-done.8) | copy-start | bytes 1572868
  372.4 6.9 %collective-permute-start.10 = (bf16[128,128]{0,1:T(8,128)(2,1)S(1)}, bf16[128,128]{0,1:T(8,128)(2,1)S(1)}, u32[]{:S(2)}, u32[]{:S(2)}) collective-permute-start(bf16[128,128]{0,1:T(8,128)(2,1)S(1)} %get-tuple-element.898), channel_id=1, source_target_pairs={{0,1},{1,2},{2,3},{3,4},{4,5},{5,6},{6,7},{7,8},{8,9},{9,10},{10,1... | collective-permute-start | bytes 98312 | tf_op jit(solution)/shard_map/ppermute | solution.py:38
  376.4 4.9 %collective-permute-start.11 = (bf16[128,128]{0,1:T(8,128)(2,1)S(1)}, bf16[128,128]{0,1:T(8,128)(2,1)S(1)}, u32[]{:S(2)}, u32[]{:S(2)}) collective-permute-start(bf16[128,128]{0,1:T(8,128)(2,1)S(1)} %get-tuple-element.899), channel_id=1, source_target_pairs={{1,0},{2,1},{3,2},{4,3},{5,4},{6,5},{7,6},{8,7},{9,8},{10,9},{11,1... | collective-permute-start | bytes 98312 | tf_op jit(solution)/shard_map/ppermute | solution.py:39
  383.9 84.9 %copy-start.4 = (f32[2048,128]{0,1:T(8,128)S(1)}, f32[2048,128]{0,1:T(8,128)}, u32[]{:S(2)}) copy-start(f32[2048,128]{0,1:T(8,128)} %copy-done.2) | copy-start | bytes 3145732
  383.9 84.9 %copy-start.6 = (f32[2048,128]{0,1:T(8,128)S(1)}, f32[2048,128]{0,1:T(8,128)}, u32[]{:S(2)}) copy-start(f32[2048,128]{0,1:T(8,128)} %copy-done.5) | copy-start | bytes 3145732
where the time goes:
time: 475 us; the launch traced here: 473 us
  blocking collectives  268 us (56%)
  local copies, waits for them, and re-layouts  72.1 us (15%)
  matrix products  47.4 us (10%)
  other arithmetic  36.1 us (8%)
  starting transfers between devices  28.4 us (6%)
  waiting for transfers between devices  14.5 us (3%)
    psum x2, blocking collectives, per_device(): lax.psum((jnp.sum(gradient * gradient), jnp.sum(projected * projected)),...  157 us
    all_gather x8, blocking collectives, entering(): everything = jax.tree.map(lambda part: lax.all_gather(part, axis), array)  111 us
    dot_general x4, matrix products, footprint_apply(): jnp.einsum('paj,pjf->paf', foot_blocks, picked, preferred_element_type=jn...  22.7 us
    unnamed x64, local copies, waits for them, and re-layouts  13.6 us
    ppermute x4, starting transfers between devices, padded(): before = lax.ppermute(last, axis, up)  13.1 us
    dot_general x8, matrix products, tri_matmul(): jnp.dot(values, table, precision=lax.Precision.HIGHEST, preferred_element...  11.4 us
    dot_general x2, local copies, waits for them, and re-layouts, footprint_apply(): jnp.einsum('paj,pjf->paf', foot_blocks, picked, preferred_element_type=jn...  11.3 us
    dot_general x2, local copies, waits for them, and re-layouts, per_device(): jnp.einsum('paj,paf->pjf', foot_blocks, residual.reshape(blocks, PIX_BLOC...  11.2 us
  transfers between devices with their start and end apart: 12, of which 6 were waited for; matrix products, arithmetic and copies ran while one was open for 4% of the time, Pallas kernels for 0%

commit v1 on v0

--- a/solution.py
+++ b/solution.py
@@ -143,7 +143,7 @@
         direction = forward_pass(drive_gain * gradient).astype(jnp.bfloat16)
         projected = footprint_apply(direction)
         grad_sq, image_sq = lax.psum(
-            (jnp.sum(gradient * gradient), jnp.sum(projected * projected)), ("tm", "tile")
+            lax.psum((jnp.sum(gradient * gradient), jnp.sum(projected * projected)), "tm"), "tile"
         )
         step_size = grad_sq / (image_sq + 1e-06)
         current = jnp.maximum(current - step_size * gradient, 0.0)

time: 475 us -> 484 us (1.019)
  the two profiles are of different devices: /device:TPU:1 before, /device:TPU:32 now
where the time goes in v1:
time: 484 us; the launch traced here: 482 us
  blocking collectives  272 us (56%)
  local copies, waits for them, and re-layouts  72.1 us (15%)
  matrix products  47.3 us (10%)
  starting transfers between devices  37.6 us (8%)
  other arithmetic  35.5 us (7%)
  waiting for transfers between devices  11.1 us (2%)
    psum x2, blocking collectives, per_device(): lax.psum(lax.psum((jnp.sum(gradient * gradient), jnp.sum(projected * proj...  142 us
    all_gather x8, blocking collectives, entering(): everything = jax.tree.map(lambda part: lax.all_gather(part, axis), array)  103 us
    psum x2, blocking collectives, per_device(): lax.psum((jnp.sum(gradient * gradient), jnp.sum(projected * projected)),...  27.3 us
    dot_general x4, matrix products, footprint_apply(): jnp.einsum('paj,pjf->paf', foot_blocks, picked, preferred_element_type=jn...  22.6 us
    ppermute x4, starting transfers between devices, shifted(): return lax.ppermute(array, axis, pairs)  13.6 us
    unnamed x64, local copies, waits for them, and re-layouts  13.6 us
    ppermute x4, starting transfers between devices, padded(): after = lax.ppermute(initial, axis, down)  12.3 us
    ppermute x4, starting transfers between devices, padded(): before = lax.ppermute(last, axis, up)  11.7 us
  transfers between devices with their start and end apart: 12, of which 6 were waited for; matrix products, arithmetic and copies ran while one was open for 4% of the time, Pallas kernels for 0%

profile of v1, /device:TPU:32, one launch (start us, length us, event | category | flops | bytes accessed | tf_op | source)
XLA Modules:
  0.0 481.5 jit_solution(1144618288119697854)
XLA Ops:
  6.4 13.2 %all-gather.1 = f32[16384,1]{0,1:T(1,128)S(1)} all-gather(f32[2048,1]{0,1:T(1,128)S(1)} %slice.222), channel_id=3, replica_groups=mesh['tm'=8,'tile'=32] {'tm'}, dimensions={0}, use_global_device_ids=true | all-gather | bytes 73728 | tf_op jit(solution)/shard_map/all_gather | solution.py:15
  20.9 12.8 %all-gather = f32[16384,1]{0,1:T(1,128)S(1)} all-gather(f32[2048,1]{0,1:T(1,128)S(1)} %slice.221), channel_id=2, replica_groups=mesh['tm'=8,'tile'=32] {'tm'}, dimensions={0}, use_global_device_ids=true | all-gather | bytes 73728 | tf_op jit(solution)/shard_map/all_gather | solution.py:15
  36.3 3.8 collective-permute-start
  46.3 2.2 gather_fusion
  48.4 6.3 %convolution_bitcast_fusion.3 = f32[32,256,128]{1,2,0:T(8,128)} fusion(bf16[32,256,128]{2,1,0:T(8,128)(2,1)} %bitcast.92, bf16[32,256,256]{2,1,0:T(8,128)(2,1)} %bitcast.82), kind=kOutput, calls=%fused_computation.38 | convolution fusion | flops 536870912 | bytes 10485760 | tf_op jit(solution)/shard_map/paj,pjf->paf/dot_general | solution.py:107
  54.7 5.6 %copy.21 = f32[32,256,128]{2,1,0:T(8,128)} copy(f32[32,256,128]{1,2,0:T(8,128)} %convolution_bitcast_fusion.3) | data formatting | bytes 8388608 | tf_op jit(solution)/shard_map/paj,pjf->paf/dot_general | solution.py:107
  60.4 3.4 fusion
  64.4 2.8 convolution_bitcast_fusion.2
  67.2 5.6 %copy.23 = f32[32,256,128]{2,1,0:T(8,128)} copy(f32[32,256,128]{1,2,0:T(8,128)} %convolution_bitcast_fusion.2) | data formatting | bytes 8388608 | tf_op jit(solution)/shard_map/paj,paf->pjf/dot_general | solution.py:116
  72.8 5.0 %reshape.231 = f32[128,8192]{1,0:T(8,128)} reshape(f32[32,256,128]{2,1,0:T(8,128)} %copy.23) | data formatting | bytes 8388608 | tf_op jit(solution)/shard_map/reshape | solution.py:122
  77.8 3.8 fusion.25
  84.0 5.1 %collective-permute-start.2 = (f32[128,128]{0,1:T(8,128)}, f32[128,128]{0,1:T(8,128)}, u32[]{:S(2)}, u32[]{:S(2)}) collective-permute-start(f32[128,128]{0,1:T(8,128)} %copy.24), channel_id=1, source_target_pairs={{0,1},{1,2},{2,3},{3,4},{4,5},{5,6},{6,7},{7,8},{8,9},{9,10},{10,1... | collective-permute-start | bytes 196616 | tf_op jit(solution)/shard_map/ppermute | solution.py:47
  94.9 2.1 collective-permute-start.3
  98.5 3.8 collective-permute-done.3
  103.8 2.2 convolution_divide_fusion.1
  106.9 12.8 %all-gather.3 = f32[16384,1]{0,1:T(1,128)S(1)} all-gather(f32[2048,1]{0,1:T(1,128)S(1)} %get-tuple-element.900), channel_id=5, replica_groups=mesh['tm'=8,'tile'=32] {'tm'}, dimensions={0}, use_global_device_ids=true | all-gather | bytes 73728 | tf_op jit(solution)/shard_map/all_gather | solution.py:15
  120.4 12.8 %all-gather.2 = f32[16384,1]{0,1:T(1,128)S(1)} all-gather(f32[2048,1]{0,1:T(1,128)S(1)} %get-tuple-element.901), channel_id=4, replica_groups=mesh['tm'=8,'tile'=32] {'tm'}, dimensions={0}, use_global_device_ids=true | all-gather | bytes 73728 | tf_op jit(solution)/shard_map/all_gather | solution.py:15
  138.2 12.8 %all-gather.4 = f32[16384,1]{0,1:T(1,128)S(1)} all-gather(f32[2048,1]{0,1:T(1,128)S(1)} %slice.234), channel_id=6, replica_groups=mesh['tm'=8,'tile'=32] {'tm'}, dimensions={0}, use_global_device_ids=true | all-gather | bytes 73728 | tf_op jit(solution)/shard_map/all_gather | solution.py:15
  153.6 3.9 collective-permute-start.4
  159.5 4.1 collective-permute-done.5
  164.0 2.2 gather_fusion.1
  166.2 5.0 %multiply_reduce_fusion.1 = f32[]{:T(128)} fusion(bf16[32,256,128]{2,1,0:T(8,128)(2,1)} %bitcast.97, bf16[32,256,256]{2,1,0:T(8,128)(2,1)} %bitcast.83), kind=kOutput, calls=%fused_computation.27 | convolution fusion | flops 538968064 | bytes 6291460 | tf_op jit(solution)/shard_map/paj,pjf->paf/dot_general | solution.py:107
  171.2 14.3 %all-reduce.4 = (f32[]{:T(128)}, f32[]{:T(128)}) all-reduce(f32[]{:T(128)} %get-tuple-element.880, f32[]{:T(128)} %multiply_reduce_fusion.1), channel_id=1, replica_groups=mesh['tm'=8,'tile'=32] {'tm'}, use_global_device_ids=true, to_apply=%region_5.6 | all-reduce | flops 2 | bytes 16 | tf_op jit(solution)/shard_map/psum | solution.py:146
  185.4 70.0 %all-reduce.2 = (f32[]{:T(128)}, f32[]{:T(128)}) all-reduce(f32[]{:T(128)} %get-tuple-element.874, f32[]{:T(128)} %get-tuple-element.875), channel_id=1, replica_groups=mesh['tm'=8,'tile'=32] {'tile'}, use_global_device_ids=true, to_apply=%region_6.7 | all-reduce | flops 2 | bytes 16 | tf_op jit(solution)/shard_map/psum | solution.py:145
  256.7 2.1 convolution_multiply_fusion.1
  259.8 12.8 %all-gather.5 = f32[16384,1]{0,1:T(1,128)S(1)} all-gather(f32[2048,1]{0,1:T(1,128)S(1)} %slice.237), channel_id=7, replica_groups=mesh['tm'=8,'tile'=32] {'tm'}, dimensions={0}, use_global_device_ids=true | all-gather | bytes 73728 | tf_op jit(solution)/shard_map/all_gather | solution.py:15
  273.8 2.4 fusion.30
  278.2 4.1 collective-permute-start.7
  284.3 2.2 gather_fusion.2
  286.5 6.3 %convolution_bitcast_fusion.1 = f32[32,256,128]{1,2,0:T(8,128)} fusion(bf16[32,256,128]{2,1,0:T(8,128)(2,1)} %bitcast.93, bf16[32,256,256]{2,1,0:T(8,128)(2,1)} %bitcast.84), kind=kOutput, calls=%fused_computation.36 | convolution fusion | flops 536870912 | bytes 10485760 | tf_op jit(solution)/shard_map/paj,pjf->paf/dot_general | solution.py:107
  292.8 5.6 %copy.33 = f32[32,256,128]{2,1,0:T(8,128)} copy(f32[32,256,128]{1,2,0:T(8,128)} %convolution_bitcast_fusion.1) | data formatting | bytes 8388608 | tf_op jit(solution)/shard_map/paj,pjf->paf/dot_general | solution.py:107
  298.4 3.4 fusion.1
  302.4 2.8 convolution_bitcast_fusion
  305.3 5.6 %copy.35 = f32[32,256,128]{2,1,0:T(8,128)} copy(f32[32,256,128]{1,2,0:T(8,128)} %convolution_bitcast_fusion) | data formatting | bytes 8388608 | tf_op jit(solution)/shard_map/paj,paf->pjf/dot_general | solution.py:116
  310.9 5.0 %reshape.239 = f32[128,8192]{1,0:T(8,128)} reshape(f32[32,256,128]{2,1,0:T(8,128)} %copy.35) | data formatting | bytes 8388608 | tf_op jit(solution)/shard_map/reshape | solution.py:122
  315.9 3.8 fusion.24
  329.6 4.5 collective-permute-start.9
  337.5 2.2 convolution_divide_fusion
  341.5 12.7 %all-gather.6 = f32[16384,1]{0,1:T(1,128)S(1)} all-gather(f32[2048,1]{0,1:T(1,128)S(1)} %slice_multiply_fusion), channel_id=8, replica_groups=mesh['tm'=8,'tile'=32] {'tm'}, dimensions={0}, use_global_device_ids=true | all-gather | bytes 73728 | tf_op jit(solution)/shard_map/all_gather | solution.py:15
  355.6 2.1 multiply_reduce_fusion.2
  359.6 12.9 %all-gather.7 = f32[16384,1]{0,1:T(1,128)S(1)} all-gather(f32[2048,1]{0,1:T(1,128)S(1)} %slice.246), channel_id=9, replica_groups=mesh['tm'=8,'tile'=32] {'tm'}, dimensions={0}, use_global_device_ids=true | all-gather | bytes 73728 | tf_op jit(solution)/shard_map/all_gather | solution.py:15
  375.9 2.1 collective-permute-start.10
  377.9 4.2 collective-permute-start.11
  384.1 2.2 gather_fusion.3
  386.3 5.0 %multiply_reduce_fusion = f32[]{:T(128)} fusion(bf16[32,256,128]{2,1,0:T(8,128)(2,1)} %bitcast.96, bf16[32,256,256]{2,1,0:T(8,128)(2,1)} %bitcast.85), kind=kOutput, calls=%fused_computation.26 | convolution fusion | flops 538968064 | bytes 6291460 | tf_op jit(solution)/shard_map/paj,pjf->paf/dot_general | solution.py:107
  391.3 13.0 %all-reduce.3 = (f32[]{:T(128)}, f32[]{:T(128)}) all-reduce(f32[]{:T(128)} %get-tuple-element.876, f32[]{:T(128)} %multiply_reduce_fusion), channel_id=1, replica_groups=mesh['tm'=8,'tile'=32] {'tm'}, use_global_device_ids=true, to_apply=%region_17.18 | all-reduce | flops 2 | bytes 16 | tf_op jit(solution)/shard_map/psum | solution.py:146
  404.3 72.1 %all-reduce.1 = (f32[]{:T(128)}, f32[]{:T(128)}) all-reduce(f32[]{:T(128)} %get-tuple-element.872, f32[]{:T(128)} %get-tuple-element.873), channel_id=1, replica_groups=mesh['tm'=8,'tile'=32] {'tile'}, use_global_device_ids=true, to_apply=%region_18.19 | all-reduce | flops 2 | bytes 16 | tf_op jit(solution)/shard_map/psum | solution.py:145
  479.0 2.5 copy.42
  (266 shorter events, 71.7 us)
Async XLA Ops:
  1.3 4.0 copy-start.25
  4.5 16.3 %copy-start.2 = (f32[2048,128]{0,1:T(8,128)}, f32[2048,128]{0,1:T(8,128)S(1)}, u32[]{:S(2)}) copy-start(f32[2048,128]{0,1:T(8,128)S(1)} %copy.30) | copy-start | bytes 3145732
  5.4 1.0 copy-start.12
  6.4 35.8 %copy-start.29 = (f32[128]{0:T(128)S(1)}, f32[128]{0:T(128)}, u32[]{:S(2)}) copy-start(f32[128]{0:T(128)} %param.30) | copy-start | bytes 1540
  6.4 35.8 %copy-start.28 = (s32[32,4]{0,1:T(4,128)S(1)}, s32[32,4]{0,1:T(4,128)}, u32[]{:S(2)}) copy-start(s32[32,4]{0,1:T(4,128)} %param.28) | copy-start | bytes 1540
  6.4 36.0 %copy-start.21 = (f32[2048]{0:T(1024)S(1)}, f32[2048]{0:T(1024)}, u32[]{:S(2)}) copy-start(f32[2048]{0:T(1024)} %param.29) | copy-start | bytes 24580
  36.3 8.8 %collective-permute-start = (bf16[128,128]{0,1:T(8,128)(2,1)S(1)}, bf16[128,128]{0,1:T(8,128)(2,1)S(1)}, u32[]{:S(2)}, u32[]{:S(2)}) collective-permute-start(bf16[128,128]{0,1:T(8,128)(2,1)S(1)} %get-tuple-element.908), channel_id=1, source_target_pairs={{0,1},{1,2},{2,3},{3,4},{4,5},{5,6},{6,7},{7,8},{8,9},{9,10},{10,1... | collective-permute-start | bytes 98312 | tf_op jit(solution)/shard_map/ppermute | solution.py:38
  40.1 5.8 %collective-permute-start.1 = (bf16[128,128]{0,1:T(8,128)(2,1)S(1)}, bf16[128,128]{0,1:T(8,128)(2,1)S(1)}, u32[]{:S(2)}, u32[]{:S(2)}) collective-permute-start(bf16[128,128]{0,1:T(8,128)(2,1)S(1)} %get-tuple-element.909), channel_id=1, source_target_pairs={{1,0},{2,1},{3,2},{4,3},{5,4},{6,5},{7,6},{8,7},{9,8},{10,9},{11,1... | collective-permute-start | bytes 98312 | tf_op jit(solution)/shard_map/ppermute | solution.py:39
  43.6 2.7 copy-start.22
  60.4 4.0 copy-start
  84.0 7.9 %copy-start.20 = (f32[2,8192]{1,0:T(2,128)S(1)}, f32[2,8192]{1,0:T(2,128)}, u32[]{:S(2)}) copy-start(f32[2,8192]{1,0:T(2,128)} %get-tuple-element.899) | copy-start | bytes 196612
  84.0 13.1 %collective-permute-start.2 = (f32[128,128]{0,1:T(8,128)}, f32[128,128]{0,1:T(8,128)}, u32[]{:S(2)}, u32[]{:S(2)}) collective-permute-start(f32[128,128]{0,1:T(8,128)} %copy.24), channel_id=1, source_target_pairs={{0,1},{1,2},{2,3},{3,4},{4,5},{5,6},{6,7},{7,8},{8,9},{9,10},{10,1... | collective-permute-start | bytes 196616 | tf_op jit(solution)/shard_map/ppermute | solution.py:47
  92.0 2.7 copy-start.17
  94.9 7.4 %collective-permute-start.3 = (f32[128,128]{0,1:T(8,128)S(1)}, f32[128,128]{0,1:T(8,128)S(1)}, u32[]{:S(2)}, u32[]{:S(2)}) collective-permute-start(f32[128,128]{0,1:T(8,128)S(1)} %copy.27), channel_id=1, source_target_pairs={{1,0},{2,1},{3,2},{4,3},{5,4},{6,5},{7,6},{8,7},{9,8},{10,9},{11,1... | collective-permute-start | bytes 196616 | tf_op jit(solution)/shard_map/ppermute | solution.py:47
  103.8 30.1 %copy-start.15 = (f32[2048]{0:T(1024)S(1)}, f32[2048]{0:T(1024)}, u32[]{:S(2)}) copy-start(f32[2048]{0:T(1024)} %custom-call.1) | copy-start | bytes 24580
  103.8 30.7 %copy-start.23 = (f32[2048,1]{0,1:T(1,128)S(1)}, f32[2048,1]{0,1:T(1,128)}, u32[]{:S(2)}) copy-start(f32[2048,1]{0,1:T(1,128)} %copy-done.22) | copy-start | bytes 24580
  103.8 30.7 %copy-start.26 = (f32[2048]{0:T(1024)S(1)}, f32[2048]{0:T(1024)}, u32[]{:S(2)}) copy-start(f32[2048]{0:T(1024)} %copy-done.25) | copy-start | bytes 24580
  135.3 1.1 copy-start.5
  137.3 1.0 copy-start.14
  153.6 5.9 %collective-permute-start.4 = (bf16[128,128]{0,1:T(8,128)(2,1)S(1)}, bf16[128,128]{0,1:T(8,128)(2,1)S(1)}, u32[]{:S(2)}, u32[]{:S(2)}) collective-permute-start(bf16[128,128]{0,1:T(8,128)(2,1)S(1)} %get-tuple-element.906), channel_id=1, source_target_pairs={{0,1},{1,2},{2,3},{3,4},{4,5},{5,6},{6,7},{7,8},{8,9},{9,10},{10,1... | collective-permute-start | bytes 98312 | tf_op jit(solution)/shard_map/ppermute | solution.py:38
  157.6 6.1 %collective-permute-start.5 = (bf16[128,128]{0,1:T(8,128)(2,1)S(1)}, bf16[128,128]{0,1:T(8,128)(2,1)S(1)}, u32[]{:S(2)}, u32[]{:S(2)}) collective-permute-start(bf16[128,128]{0,1:T(8,128)(2,1)S(1)} %get-tuple-element.907), channel_id=1, source_target_pairs={{1,0},{2,1},{3,2},{4,3},{5,4},{6,5},{7,6},{8,7},{9,8},{10,9},{11,1... | collective-permute-start | bytes 98312 | tf_op jit(solution)/shard_map/ppermute | solution.py:39
  166.2 90.5 %copy-start.3 = (f32[2048,128]{0,1:T(8,128)S(1)}, f32[2048,128]{0,1:T(8,128)}, u32[]{:S(2)}) copy-start(f32[2048,128]{0,1:T(8,128)} %copy-done.2) | copy-start | bytes 3145732
  258.8 1.0 copy-start.10
  276.2 6.1 %collective-permute-start.6 = (bf16[128,128]{0,1:T(8,128)(2,1)S(1)}, bf16[128,128]{0,1:T(8,128)(2,1)S(1)}, u32[]{:S(2)}, u32[]{:S(2)}) collective-permute-start(bf16[128,128]{0,1:T(8,128)(2,1)S(1)} %get-tuple-element.904), channel_id=1, source_target_pairs={{0,1},{1,2},{2,3},{3,4},{4,5},{5,6},{6,7},{7,8},{8,9},{9,10},{10,1... | collective-permute-start | bytes 98312 | tf_op jit(solution)/shard_map/ppermute | solution.py:38
  278.2 5.8 %collective-permute-start.7 = (bf16[128,128]{0,1:T(8,128)(2,1)S(1)}, bf16[128,128]{0,1:T(8,128)(2,1)S(1)}, u32[]{:S(2)}, u32[]{:S(2)}) collective-permute-start(bf16[128,128]{0,1:T(8,128)(2,1)S(1)} %get-tuple-element.905), channel_id=1, source_target_pairs={{1,0},{2,1},{3,2},{4,3},{5,4},{6,5},{7,6},{8,7},{9,8},{10,9},{11,1... | collective-permute-start | bytes 98312 | tf_op jit(solution)/shard_map/ppermute | solution.py:39
  298.4 4.0 copy-start.1
  323.5 10.6 %collective-permute-start.8 = (f32[128,128]{0,1:T(8,128)}, f32[128,128]{0,1:T(8,128)}, u32[]{:S(2)}, u32[]{:S(2)}) collective-permute-start(f32[128,128]{0,1:T(8,128)} %copy.36), channel_id=1, source_target_pairs={{0,1},{1,2},{2,3},{3,4},{4,5},{5,6},{6,7},{7,8},{8,9},{9,10},{10,1... | collective-permute-start | bytes 196616 | tf_op jit(solution)/shard_map/ppermute | solution.py:47
  326.5 2.8 copy-start.19
  326.5 2.9 copy-start.18
  329.6 6.4 %collective-permute-start.9 = (f32[128,128]{0,1:T(8,128)S(1)}, f32[128,128]{0,1:T(8,128)S(1)}, u32[]{:S(2)}, u32[]{:S(2)}) collective-permute-start(f32[128,128]{0,1:T(8,128)S(1)} %copy.39), channel_id=1, source_target_pairs={{1,0},{2,1},{3,2},{4,3},{5,4},{6,5},{7,6},{8,7},{9,8},{10,9},{11,1... | collective-permute-start | bytes 196616 | tf_op jit(solution)/shard_map/ppermute | solution.py:47
  337.5 17.5 %copy-start.16 = (f32[2048]{0:T(1024)S(1)}, f32[2048]{0:T(1024)}, u32[]{:S(2)}) copy-start(f32[2048]{0:T(1024)} %custom-call.4) | copy-start | bytes 24580
  337.5 18.1 %copy-start.24 = (f32[2048,1]{0,1:T(1,128)S(1)}, f32[2048,1]{0,1:T(1,128)}, u32[]{:S(2)}) copy-start(f32[2048,1]{0,1:T(1,128)} %copy-done.22) | copy-start | bytes 24580
  337.5 18.1 %copy-start.27 = (f32[2048]{0:T(1024)S(1)}, f32[2048]{0:T(1024)}, u32[]{:S(2)}) copy-start(f32[2048]{0:T(1024)} %copy-done.25) | copy-start | bytes 24580
  339.7 1.0 copy-start.11
  358.6 1.0 copy-start.13
  359.5 22.6 %copy-start.7 = (f32[2048,128]{0,1:T(8,128)S(1)}, f32[2048,128]{0,1:T(8,128)}, u32[]{:S(2)}) copy-start(f32[2048,128]{0,1:T(8,128)} %get-tuple-element.879) | copy-start | bytes 3145732
  375.1 0.8 copy-start.8
  375.9 7.9 %copy-start.9 = (bf16[2048,128]{0,1:T(8,128)(2,1)S(1)}, bf16[2048,128]{0,1:T(8,128)(2,1)}, u32[]{:S(2)}) copy-start(bf16[2048,128]{0,1:T(8,128)(2,1)} %copy-done.8) | copy-start | bytes 1572868
  375.9 7.6 %collective-permute-start.10 = (bf16[128,128]{0,1:T(8,128)(2,1)S(1)}, bf16[128,128]{0,1:T(8,128)(2,1)S(1)}, u32[]{:S(2)}, u32[]{:S(2)}) collective-permute-start(bf16[128,128]{0,1:T(8,128)(2,1)S(1)} %get-tuple-element.902), channel_id=1, source_target_pairs={{0,1},{1,2},{2,3},{3,4},{4,5},{5,6},{6,7},{7,8},{8,9},{9,10},{10,1... | collective-permute-start | bytes 98312 | tf_op jit(solution)/shard_map/ppermute | solution.py:38
  377.9 5.8 %collective-permute-start.11 = (bf16[128,128]{0,1:T(8,128)(2,1)S(1)}, bf16[128,128]{0,1:T(8,128)(2,1)S(1)}, u32[]{:S(2)}, u32[]{:S(2)}) collective-permute-start(bf16[128,128]{0,1:T(8,128)(2,1)S(1)} %get-tuple-element.903), channel_id=1, source_target_pairs={{1,0},{2,1},{3,2},{4,3},{5,4},{6,5},{7,6},{8,7},{9,8},{10,9},{11,1... | collective-permute-start | bytes 98312 | tf_op jit(solution)/shard_map/ppermute | solution.py:39
  386.3 91.5 %copy-start.4 = (f32[2048,128]{0,1:T(8,128)S(1)}, f32[2048,128]{0,1:T(8,128)}, u32[]{:S(2)}) copy-start(f32[2048,128]{0,1:T(8,128)} %copy-done.2) | copy-start | bytes 3145732
  386.3 91.5 %copy-start.6 = (f32[2048,128]{0,1:T(8,128)S(1)}, f32[2048,128]{0,1:T(8,128)}, u32[]{:S(2)}) copy-start(f32[2048,128]{0,1:T(8,128)} %copy-done.5) | copy-start | bytes 3145732
